TPU v7x, 32 devices: a whole 2x2x4 slice. The times are simulated.
32 devices in a mesh: replica: 4 (over x, core), expert: 8 (over z, y).
Axes of the slice: x: 2, y: 2, z: 4, core: 2. Of those that a mesh axis runs over, the one named last changes fastest.
Arguments:
- tokens: bfloat16 [4096, 2048], P(('replica', 'expert')), may hold values from -6 to 6
- routing: int32 [4096, 8], P(('replica', 'expert')), may hold values from 0 to 7, all different within a row; in each aligned block of 128 rows (0 to 127, 128 to 255, ...) at most 128 rows name the same one
- gate_scores: float32 [4096, 8], P(('replica', 'expert')), may hold values from 0.1 to 1
- cotangent: bfloat16 [4096, 2048], P(('replica', 'expert')), may hold values from -48 to 48
- w_gate: bfloat16 [4, 8, 2048, 384], P('replica', 'expert'), may hold values from -6 to 6
- w_up: bfloat16 [4, 8, 2048, 384], P('replica', 'expert'), may hold values from -6 to 6
- w_down: bfloat16 [4, 8, 384, 2048], P('replica', 'expert'), may hold values from -6 to 6
- mom_gate: bfloat16 [4, 8, 2048, 384], P('replica', 'expert'), may hold values from -3 to 3
- mom_up: bfloat16 [4, 8, 2048, 384], P('replica', 'expert'), may hold values from -3 to 3
- mom_down: bfloat16 [4, 8, 384, 2048], P('replica', 'expert'), may hold values from -3 to 3
- gossip_round: int32 [8], P('expert'), may hold values from 0 to 1
Outputs:
- layer_out: bfloat16 [4096, 2048], P(('replica', 'expert'))
- token_grad: bfloat16 [4096, 2048], P(('replica', 'expert'))
- new_gate: bfloat16 [4, 8, 2048, 384], P('replica', 'expert')
- new_up: bfloat16 [4, 8, 2048, 384], P('replica', 'expert')
- new_down: bfloat16 [4, 8, 384, 2048], P('replica', 'expert')
- new_mom_gate: bfloat16 [4, 8, 2048, 384], P('replica', 'expert')
- new_mom_up: bfloat16 [4, 8, 2048, 384], P('replica', 'expert')
- new_mom_down: bfloat16 [4, 8, 384, 2048], P('replica', 'expert')
Inputs may be any that keep to these rules, and one draw needn't show every extreme that they name: `routing`: each token names 8 different experts; among the 128 tokens of one source no expert is named more than 128 times, a bound that some block reaches. `gossip_round`: each expert's round value names the bit distance of that expert's partner in this round.
All inputs are finite; a program needn't handle non-finite values.
Results may differ from a plain program's by a relative error of at most 0.0064.
Values may be sent and summed in bfloat16 or wider, within the bound.
No kernel may reach another device: no remote copies, remote signals or barrier semaphores. Data moves between devices by JAX's collectives and lax.ppermute only.
A program may use at most 192 MiB of HBM per device.

v0:
```python
import jax
import jax.numpy as jnp
from jax import lax
from jax.sharding import PartitionSpec as P

momentum_beta = 0.9
learn_rate = 0.1


def partner_2(value, axis, stride):
    mask = 2**stride
    pairs = [(source, source ^ mask) for source in range(lax.axis_size(axis))]
    return lax.ppermute(value, axis, pairs)


def expert_forward(rows_in, weight_gate, weight_up, weight_down):
    scale_in = rows_in.shape[1] ** (-0.5)
    scale_hidden = weight_gate.shape[1] ** (-0.5)
    gate_pre = jnp.dot(rows_in, weight_gate, preferred_element_type=jnp.float32) * scale_in
    up_pre = jnp.dot(rows_in, weight_up, preferred_element_type=jnp.float32) * scale_in
    sigmoid_gate = jax.nn.sigmoid(gate_pre)
    activation = (gate_pre * sigmoid_gate * up_pre).astype(jnp.bfloat16)
    produced = (
        jnp.dot(activation, weight_down, preferred_element_type=jnp.float32) * scale_hidden
    ).astype(jnp.bfloat16)
    return (gate_pre, up_pre, sigmoid_gate, activation, produced)


def expert_backward(
    rows_in,
    rows_grad,
    weight_gate,
    weight_up,
    weight_down,
    gate_pre,
    up_pre,
    sigmoid_gate,
    activation,
):
    scale_in = rows_in.shape[1] ** (-0.5)
    scale_hidden = weight_gate.shape[1] ** (-0.5)
    inner_dims = (((1,), (1,)), ((), ()))
    outer_dims = (((0,), (0,)), ((), ()))
    grad_act = (
        lax.dot_general(rows_grad, weight_down, inner_dims, preferred_element_type=jnp.float32)
        * scale_hidden
    )
    grad_gate_pre = (
        grad_act * up_pre * sigmoid_gate * (1.0 + gate_pre * (1.0 - sigmoid_gate))
    ).astype(jnp.bfloat16)
    grad_up_pre = (grad_act * gate_pre * sigmoid_gate).astype(jnp.bfloat16)
    grad_down = (
        lax.dot_general(activation, rows_grad, outer_dims, preferred_element_type=jnp.float32)
        * scale_hidden
    )
    grad_gate = (
        lax.dot_general(rows_in, grad_gate_pre, outer_dims, preferred_element_type=jnp.float32)
        * scale_in
    )
    grad_up = (
        lax.dot_general(rows_in, grad_up_pre, outer_dims, preferred_element_type=jnp.float32)
        * scale_in
    )
    back_sum = lax.dot_general(
        grad_gate_pre, weight_gate, inner_dims, preferred_element_type=jnp.float32
    )
    back_sum = back_sum + lax.dot_general(
        grad_up_pre, weight_up, inner_dims, preferred_element_type=jnp.float32
    )
    rows_back = (back_sum * scale_in).astype(jnp.bfloat16)
    return (rows_back, grad_gate, grad_up, grad_down)


def momentum_step(weight, moment, gradient):
    moment_new = momentum_beta * moment.astype(jnp.float32) + gradient
    weight_new = (weight.astype(jnp.float32) - learn_rate * moment_new).astype(jnp.bfloat16)
    return (weight_new, moment_new.astype(jnp.bfloat16))


def per_device_routed(
    tokens,
    routing,
    gate_scores,
    cotangent,
    w_gate,
    w_up,
    w_down,
    mom_gate,
    mom_up,
    mom_down,
    gossip_round,
):
    tok_rows, feature_width = tokens.shape
    top_count = routing.shape[1]
    experts = lax.axis_size("expert")
    capacity = max(2, min(tok_rows, tok_rows * top_count // experts + 8))
    gate_share = gate_scores / jnp.sum(gate_scores, axis=1, keepdims=True)
    expert_ids = routing.reshape(-1)
    member = (expert_ids[:, None] == jnp.arange(experts, dtype=jnp.int32)[None, :]).astype(
        jnp.int32
    )
    earlier = jnp.sum((jnp.cumsum(member, axis=0) - member) * member, axis=1)
    target = expert_ids * capacity + earlier
    source = jnp.arange(expert_ids.shape[0], dtype=jnp.int32) // top_count
    send_rows = (
        jnp.zeros((experts * capacity, feature_width), jnp.bfloat16).at[target].set(tokens[source])
    )
    weighted = (gate_share.reshape(-1)[:, None] * cotangent[source].astype(jnp.float32)).astype(
        jnp.bfloat16
    )
    send_grad = (
        jnp.zeros((experts * capacity, feature_width), jnp.bfloat16).at[target].set(weighted)
    )
    arrived = lax.all_to_all(
        send_rows.reshape(experts, capacity, feature_width),
        "expert",
        split_axis=0,
        concat_axis=0,
        tiled=True,
    ).reshape(-1, feature_width)
    arrived_grad = lax.all_to_all(
        send_grad.reshape(experts, capacity, feature_width),
        "expert",
        split_axis=0,
        concat_axis=0,
        tiled=True,
    ).reshape(-1, feature_width)
    weight_gate = w_gate[0, 0]
    weight_up = w_up[0, 0]
    weight_down = w_down[0, 0]
    gate_pre, up_pre, sigmoid_gate, activation, produced = expert_forward(
        arrived, weight_gate, weight_up, weight_down
    )
    returned = lax.all_to_all(
        produced.reshape(experts, capacity, feature_width),
        "expert",
        split_axis=0,
        concat_axis=0,
        tiled=True,
    ).reshape(-1, feature_width)
    picked = returned[target].astype(jnp.float32) * gate_share.reshape(-1)[:, None]
    layer_out = jnp.sum(picked.reshape(tok_rows, top_count, feature_width), axis=1).astype(
        jnp.bfloat16
    )
    rows_back, grad_gate, grad_up, grad_down = expert_backward(
        arrived,
        arrived_grad,
        weight_gate,
        weight_up,
        weight_down,
        gate_pre,
        up_pre,
        sigmoid_gate,
        activation,
    )
    returned_grad = lax.all_to_all(
        rows_back.reshape(experts, capacity, feature_width),
        "expert",
        split_axis=0,
        concat_axis=0,
        tiled=True,
    ).reshape(-1, feature_width)
    picked_back = returned_grad[target].astype(jnp.float32)
    token_grad = jnp.sum(picked_back.reshape(tok_rows, top_count, feature_width), axis=1).astype(
        jnp.bfloat16
    )
    gate_new, gate_moment = momentum_step(weight_gate, mom_gate[0, 0], grad_gate)
    up_new, up_moment = momentum_step(weight_up, mom_up[0, 0], grad_up)
    down_new, down_moment = momentum_step(weight_down, mom_down[0, 0], grad_down)
    hidden_width = weight_gate.shape[1]
    stacked = jnp.stack([gate_new, up_new, down_new.reshape(feature_width, hidden_width)], axis=0)
    bit_count = lax.axis_size("replica").bit_length() - 1
    bit_now = gossip_round[0] % bit_count
    partner = stacked
    for bit_index in range(bit_count):
        swapped = partner_2(stacked, "replica", bit_index)
        partner = jnp.where(bit_now == bit_index, swapped, partner)
    averaged = ((stacked.astype(jnp.float32) + partner.astype(jnp.float32)) * 0.5).astype(
        jnp.bfloat16
    )
    new_gate = averaged[0][None, None]
    new_up = averaged[1][None, None]
    new_down = averaged[2].reshape(hidden_width, feature_width)[None, None]
    return (
        layer_out,
        token_grad,
        new_gate,
        new_up,
        new_down,
        gate_moment[None, None],
        up_moment[None, None],
        down_moment[None, None],
    )


def ring_order(experts):
    return list(range(0, experts, 2)) + list(range(experts - 1, 0, -2))


def ring_hop(value, experts, step):
    order = ring_order(experts)
    pairs = [(order[i], order[(i + step) % experts]) for i in range(experts)]
    return lax.ppermute(value, "expert", pairs)


def after(value, *others):
    return lax.optimization_barrier((value,) + others)[0]


def ring_gather_pair(first, second, table, experts):
    half = first.shape[0] // 2
    last = experts // 2
    blocks = [[None] * experts, [None] * experts]
    moving = [(first, first), (second, second)]
    table = table[None]
    for which, own in enumerate((first, second)):
        blocks[which][0] = own
    for step in range(1, last):
        swapped = None
        if table.shape[0] < experts:
            bit = table.shape[0]
            pairs = [(e, e ^ bit) for e in range(experts)]
            swapped = lax.ppermute(table, "expert", pairs)
        for which in range(2):
            behind, ahead = moving[which]
            behind = ring_hop(behind, experts, 1)
            ahead = ring_hop(ahead, experts, -1)
            if which == 0:
                moving[0] = lax.optimization_barrier((behind, ahead))
                if swapped is not None:
                    table = jnp.concatenate([table, after(swapped, moving[0])], axis=0)
            else:
                moving[1] = after((behind, ahead), moving[0], table)
            blocks[which][experts - step], blocks[which][step] = moving[which]
    for which in range(2):
        behind, ahead = moving[which]
        top = ring_hop(behind[:half], experts, 1)
        bottom = ring_hop(ahead[half:], experts, -1)
        blocks[which][last] = jnp.concatenate([top, bottom], axis=0)
    while table.shape[0] < experts:
        bit = table.shape[0]
        pairs = [(e, e ^ bit) for e in range(experts)]
        table = jnp.concatenate([table, lax.ppermute(table, "expert", pairs)], axis=0)
    return blocks, table


def ring_scatter(parts, experts, gate):
    half = parts[0].shape[0] // 2
    last = experts // 2
    f32 = jnp.float32
    forward = ring_hop(parts[last][:half].astype(jnp.bfloat16), experts, 1)
    backward = ring_hop(parts[last][half:].astype(jnp.bfloat16), experts, -1)
    for step in range(last - 1, 0, -1):
        mine_f, mine_b = parts[step], parts[experts - step]
        if step == last - 1:
            add_f = jnp.concatenate([mine_f[:half] + forward.astype(f32), mine_f[half:]], axis=0)
            add_b = jnp.concatenate([mine_b[:half], mine_b[half:] + backward.astype(f32)], axis=0)
        else:
            add_f = mine_f + forward.astype(f32)
            add_b = mine_b + backward.astype(f32)
        add_f, add_b = add_f.astype(jnp.bfloat16), add_b.astype(jnp.bfloat16)
        add_f, add_b = after((add_f, add_b), gate(step, forward, backward))
        forward = ring_hop(add_f, experts, 1)
        backward = ring_hop(add_b, experts, -1)
    total = parts[0] + forward.astype(f32) + backward.astype(f32)
    return total.astype(jnp.bfloat16)


def share_table(routing, gate_share, experts):
    ids = jnp.arange(experts, dtype=jnp.int32)
    names = routing[:, None, :] == ids[None, :, None]
    return jnp.sum(jnp.where(names, gate_share[:, None, :], 0.0), axis=2).T


def own_shares(tables, experts):
    me = lax.axis_index("expert")
    ids = jnp.arange(experts, dtype=jnp.int32)
    order = ring_order(experts)
    away = [[order[(order.index(e) + j) % experts] ^ e for j in range(experts)] for e in range(experts)]
    mine = jnp.sum(jnp.where((ids == me)[None, :, None], tables, 0.0), axis=1)
    picks = jnp.array(away, dtype=jnp.int32)[me]
    rows = jnp.sum(jnp.where(picks[:, None, None] == ids[None, :, None], mine[None], 0.0), axis=1)
    return [rows[j][:, None] for j in range(experts)]


def per_device_dense(
    tokens,
    routing,
    gate_scores,
    cotangent,
    w_gate,
    w_up,
    w_down,
    mom_gate,
    mom_up,
    mom_down,
    gossip_round,
):
    tok_rows, feature_width = tokens.shape
    experts = lax.axis_size("expert")
    weight_gate = w_gate[0, 0]
    weight_up = w_up[0, 0]
    weight_down = w_down[0, 0]
    hidden_width = weight_gate.shape[1]
    scale_in = feature_width ** (-0.5)
    scale_hidden = hidden_width ** (-0.5)
    inner_dims = (((1,), (1,)), ((), ()))
    outer_dims = (((0,), (0,)), ((), ()))
    gate_share = gate_scores / jnp.sum(gate_scores, axis=1, keepdims=True)
    table = share_table(routing, gate_share, experts)
    blocks, tables = ring_gather_pair(tokens, cotangent, table, experts)
    tok_blocks, cot_blocks = blocks
    share_blocks = own_shares(after(tables, tok_blocks[experts // 2]), experts)
    weight_both = jnp.concatenate([weight_gate, weight_up], axis=1)

    arrival = [0]
    for step in range(1, experts // 2):
        arrival = arrival + [step, experts - step]
    arrival.append(experts // 2)

    acts, gate_grads, up_grads = [], [], []
    for place in arrival:
        block, cot, share = tok_blocks[place], cot_blocks[place], share_blocks[place]
        both_pre = jnp.dot(block, weight_both, preferred_element_type=jnp.float32) * scale_in
        gate_pre = both_pre[:, :hidden_width]
        up_pre = both_pre[:, hidden_width:]
        sigmoid_gate = jax.nn.sigmoid(gate_pre)
        acts.append((gate_pre * sigmoid_gate * up_pre * share).astype(jnp.bfloat16))
        grad_act = lax.dot_general(
            cot, weight_down, inner_dims, preferred_element_type=jnp.float32
        ) * (share * scale_hidden)
        gate_grads.append(
            (grad_act * up_pre * sigmoid_gate * (1.0 + gate_pre * (1.0 - sigmoid_gate))).astype(
                jnp.bfloat16
            )
        )
        up_grads.append((grad_act * gate_pre * sigmoid_gate).astype(jnp.bfloat16))
    rows_in = jnp.concatenate([tok_blocks[place] for place in arrival], axis=0)
    rows_cot = jnp.concatenate([cot_blocks[place] for place in arrival], axis=0)
    activation = jnp.concatenate(acts, axis=0)
    both_grads = [jnp.concatenate(pair, axis=1) for pair in zip(gate_grads, up_grads)]
    grad_gate_pre = jnp.concatenate(gate_grads, axis=0)
    grad_up_pre = jnp.concatenate(up_grads, axis=0)

    bit_count = lax.axis_size("replica").bit_length() - 1
    bit_now = gossip_round[0] % bit_count

    def swap(local, bit_index, *others):
        return partner_2(after(local, *others) if others else local, "replica", bit_index)

    def mean(one, other):
        total = one.astype(jnp.float32) + other.astype(jnp.float32)
        return (total * 0.5).astype(jnp.bfloat16)

    def with_near(local, swapped):
        result = local
        for bit_index, value in enumerate(swapped):
            result = jnp.where(bit_now == bit_index, mean(local, value), result)
        return lax.optimization_barrier(result)

    def with_far(base, value):
        return jnp.where(bit_now == bit_count - 1, mean(base, value), base)

    def averaged(local, swapped):
        return with_far(with_near(local, swapped[:-1]), swapped[-1])

    grad_down = (
        lax.dot_general(activation, rows_cot, outer_dims, preferred_element_type=jnp.float32)
        * scale_hidden
    )
    down_new, down_moment = momentum_step(weight_down, mom_down[0, 0], grad_down)
    def parts_of(place, *others):
        act, both_grad = after((acts_of[place], both_grads_of[place]), *others)
        out_part = jnp.dot(act, weight_down, preferred_element_type=jnp.float32) * scale_hidden
        back_part = (
            lax.dot_general(both_grad, weight_both, inner_dims, preferred_element_type=jnp.float32)
            * scale_in
        )
        return lax.optimization_barrier(out_part), lax.optimization_barrier(back_part)

    acts_of = dict(zip(arrival, acts))
    both_grads_of = dict(zip(arrival, both_grads))
    first = experts // 2
    out_parts = [None] * experts
    back_parts = [None] * experts
    out_parts[first], back_parts[first] = parts_of(first, down_new)
    grad_gate_pre, grad_up_pre = after(
        (grad_gate_pre, grad_up_pre), out_parts[first], back_parts[first]
    )
    grad_gate = (
        lax.dot_general(rows_in, grad_gate_pre, outer_dims, preferred_element_type=jnp.float32)
        * scale_in
    )
    grad_up = (
        lax.dot_general(rows_in, grad_up_pre, outer_dims, preferred_element_type=jnp.float32)
        * scale_in
    )
    gate_new, gate_moment = momentum_step(weight_gate, mom_gate[0, 0], grad_gate)
    up_new, up_moment = momentum_step(weight_up, mom_up[0, 0], grad_up)
    both_new = jnp.concatenate([gate_new, up_new], axis=0)
    for place in arrival:
        if place != first:
            out_parts[place], back_parts[place] = parts_of(place, down_new, out_parts[first], back_parts[first])

    far = bit_count - 1
    down_far = swap(down_new, far)
    both_far = swap(both_new, far)
    down_near = [swap(down_new, bit_index) for bit_index in range(far)]
    both_near = [swap(both_new, bit_index, down_far) for bit_index in range(far)]

    def gate(step, forward, backward):
        if step == 3:
            return (both_new, down_near)
        if step == 2:
            return (down_far,)
        return ()

    parts = [
        jnp.concatenate([out_part, back_part], axis=0)
        for out_part, back_part in zip(out_parts, back_parts)
    ]
    returns = ring_scatter(parts, experts, gate)
    layer_out, token_grad = returns[:tok_rows], returns[tok_rows:]

    new_down = averaged(down_new, down_near + [down_far])
    both_base = with_near(both_new, both_near)
    new_gate = with_far(both_base[:feature_width], both_far[:feature_width])
    new_up = with_far(both_base[feature_width:], both_far[feature_width:])
    return (
        layer_out,
        token_grad,
        new_gate[None, None],
        new_up[None, None],
        new_down[None, None],
        gate_moment[None, None],
        up_moment[None, None],
        down_moment[None, None],
    )


def per_device(tokens, routing, *others):
    if routing.shape[1] == lax.axis_size("expert"):
        return per_device_dense(tokens, routing, *others)
    return per_device_routed(tokens, routing, *others)


def solution(mesh):
    placed = (
        P(("replica", "expert"), None),
        P(("replica", "expert"), None),
        P(("replica", "expert"), None),
        P(("replica", "expert"), None),
        P("replica", "expert", None, None),
        P("replica", "expert", None, None),
        P("replica", "expert", None, None),
        P("replica", "expert", None, None),
        P("replica", "expert", None, None),
        P("replica", "expert", None, None),
        P("expert"),
    )
    return jax.shard_map(
        per_device,
        mesh=mesh,
        in_specs=placed,
        out_specs=(
            P(("replica", "expert"), None),
            P(("replica", "expert"), None),
            P("replica", "expert", None, None),
            P("replica", "expert", None, None),
            P("replica", "expert", None, None),
            P("replica", "expert", None, None),
            P("replica", "expert", None, None),
            P("replica", "expert", None, None),
        ),
        check_vma=False,
    )
```

profile of v0, /device:TPU:0, one launch (start us, length us, event | category | flops | bytes accessed | tf_op | source)
XLA Modules:
  0.0 205.9 jit_solution(12610525394348786835)
XLA Ops:
  0.6 3.1 %collective-permute-start.1 = (bf16[128,2048]{1,0:T(8,128)(2,1)}, bf16[128,2048]{1,0:T(8,128)(2,1)S(1)}, u32[]{:S(2)}, u32[]{:S(2)}) collective-permute-start(bf16[128,2048]{1,0:T(8,128)(2,1)} %param.12), channel_id=1, source_target_pairs={{0,2},{2,4},{4,6},{6,7},{7,5},{5,3},{3,1},{1,0},{8,10},{10,12},{12... | collective-permute-start | bytes 1572872 | tf_op jit(solution)/shard_map/ppermute | solution.py:203
  3.7 2.0 collective-permute-start.11
  7.8 2.0 collective-permute-start
  9.9 1.9 constant_dynamic-update-slice_fusion.18
  12.4 2.7 %fusion.38 = f32[128,768]{1,0:T(8,128)S(1)} fusion(bf16[128,2048]{1,0:T(8,128)(2,1)} %param.12, bf16[2048,384]{1,0:T(8,128)(2,1)} %bitcast.176, bf16[2048,384]{1,0:T(8,128)(2,1)} %bitcast.192), kind=kOutput, calls=%fused_computation.76 | convolution fusion | flops 409042944 | bytes 4063232 | tf_op jit(solution)/shard_map/dot_general | solution.py:324
  16.7 2.0 collective-permute-done.2
  20.8 7.1 %collective-permute-done = f32[1,8,128]{2,1,0:T(8,128)S(1)} collective-permute-done((f32[1,8,128]{2,1,0:T(8,128)S(1)}, f32[1,8,128]{2,1,0:T(8,128)S(1)}, u32[]{:S(2)}, u32[]{:S(2)}) %collective-permute-start) | collective-permute-done | bytes 4128 | tf_op jit(solution)/shard_map/ppermute | solution.py:223
  28.0 2.6 %convolution_multiply_fusion.23 = f32[128,768]{1,0:T(8,128)S(1)} fusion(bf16[128,2048]{1,0:T(8,128)(2,1)S(1)} %collective-permute-done.2, bf16[2048,384]{1,0:T(8,128)(2,1)} %bitcast.177, bf16[2048,384]{1,0:T(8,128)(2,1)} %bitcast.193), kind=kOutput, calls=%fused_computation.83 | convolution fusion | flops 409042944 | bytes 4063232 | tf_op jit(solution)/shard_map/dot_general | solution.py:324
  30.6 1.9 collective-permute-start.13
  33.0 2.6 %convolution_multiply_fusion.22 = f32[128,768]{1,0:T(8,128)S(1)} fusion(bf16[128,2048]{1,0:T(8,128)(2,1)S(1)} %collective-permute-done.1, bf16[2048,384]{1,0:T(8,128)(2,1)} %bitcast.178, bf16[2048,384]{1,0:T(8,128)(2,1)} %bitcast.194), kind=kOutput, calls=%fused_computation.82 | convolution fusion | flops 409042944 | bytes 4063232 | tf_op jit(solution)/shard_map/dot_general | solution.py:324
  35.7 3.5 %collective-permute-done.4 = bf16[128,2048]{1,0:T(8,128)(2,1)S(1)} collective-permute-done((bf16[128,2048]{1,0:T(8,128)(2,1)S(1)}, bf16[128,2048]{1,0:T(8,128)(2,1)S(1)}, u32[]{:S(2)}, u32[]{:S(2)}) %collective-permute-start.4) | collective-permute-done | bytes 524320 | tf_op jit(solution)/shard_map/ppermute | solution.py:203
  39.2 2.1 %collective-permute-done.5 = bf16[128,2048]{1,0:T(8,128)(2,1)S(1)} collective-permute-done((bf16[128,2048]{1,0:T(8,128)(2,1)S(1)}, bf16[128,2048]{1,0:T(8,128)(2,1)S(1)}, u32[]{:S(2)}, u32[]{:S(2)}) %collective-permute-start.5) | collective-permute-done | bytes 524320 | tf_op jit(solution)/shard_map/ppermute | solution.py:203
  43.3 2.6 %collective-permute-start.6 = (f32[4,8,128]{2,1,0:T(8,128)S(1)}, f32[4,8,128]{2,1,0:T(8,128)S(1)}, u32[]{:S(2)}, u32[]{:S(2)}) collective-permute-start(f32[4,8,128]{2,1,0:T(8,128)S(1)} %pad_maximum_fusion.13), channel_id=1, source_target_pairs={{0,4},{1,5},{2,6},{3,7},{4,0},{5,1},{6,2},{7,3},{8,12},{9,13},{10,... | collective-permute-start | bytes 49160 | tf_op jit(solution)/shard_map/ppermute | solution.py:223
  46.5 3.9 %collective-permute-done.13 = bf16[128,2048]{1,0:T(8,128)(2,1)S(1)} collective-permute-done((bf16[128,2048]{1,0:T(8,128)(2,1)S(1)}, bf16[128,2048]{1,0:T(8,128)(2,1)S(1)}, u32[]{:S(2)}, u32[]{:S(2)}) %collective-permute-start.13) | collective-permute-done | bytes 524320 | tf_op jit(solution)/shard_map/ppermute | solution.py:203
  50.4 2.2 %collective-permute-done.14 = bf16[128,2048]{1,0:T(8,128)(2,1)S(1)} collective-permute-done((bf16[128,2048]{1,0:T(8,128)(2,1)S(1)}, bf16[128,2048]{1,0:T(8,128)(2,1)S(1)}, u32[]{:S(2)}, u32[]{:S(2)}) %collective-permute-start.14) | collective-permute-done | bytes 524320 | tf_op jit(solution)/shard_map/ppermute | solution.py:203
  52.7 2.1 %collective-permute-start.15 = (bf16[128,2048]{1,0:T(8,128)(2,1)S(1)}, bf16[128,2048]{1,0:T(8,128)(2,1)S(1)}, u32[]{:S(2)}, u32[]{:S(2)}) collective-permute-start(bf16[128,2048]{1,0:T(8,128)(2,1)S(1)} %collective-permute-done.13), channel_id=1, source_target_pairs={{0,2},{2,4},{4,6},{6,7},{7,5},{5,3},{3,1},{1,0},{8,10},{10,12},{12... | collective-permute-start | bytes 1572872 | tf_op jit(solution)/shard_map/ppermute | solution.py:203
  55.5 6.1 %collective-permute-done.7 = bf16[128,2048]{1,0:T(8,128)(2,1)S(1)} collective-permute-done((bf16[128,2048]{1,0:T(8,128)(2,1)S(1)}, bf16[128,2048]{1,0:T(8,128)(2,1)S(1)}, u32[]{:S(2)}, u32[]{:S(2)}) %collective-permute-start.7) | collective-permute-done | bytes 524320 | tf_op jit(solution)/shard_map/ppermute | solution.py:203
  61.6 2.4 %collective-permute-done.8 = bf16[128,2048]{1,0:T(8,128)(2,1)S(1)} collective-permute-done((bf16[128,2048]{1,0:T(8,128)(2,1)S(1)}, bf16[128,2048]{1,0:T(8,128)(2,1)S(1)}, u32[]{:S(2)}, u32[]{:S(2)}) %collective-permute-start.8) | collective-permute-done | bytes 524320 | tf_op jit(solution)/shard_map/ppermute | solution.py:203
  66.5 5.5 %collective-permute-done.15 = bf16[128,2048]{1,0:T(8,128)(2,1)S(1)} collective-permute-done((bf16[128,2048]{1,0:T(8,128)(2,1)S(1)}, bf16[128,2048]{1,0:T(8,128)(2,1)S(1)}, u32[]{:S(2)}, u32[]{:S(2)}) %collective-permute-start.15) | collective-permute-done | bytes 524320 | tf_op jit(solution)/shard_map/ppermute | solution.py:203
  72.1 2.0 collective-permute-done.16
  74.2 1.8 collective-permute-start.17
  78.6 8.1 %collective-permute-done.9 = bf16[64,2048]{1,0:T(8,128)(2,1)S(1)} collective-permute-done((bf16[64,2048]{1,0:T(8,128)(2,1)S(1)}, bf16[64,2048]{1,0:T(8,128)(2,1)S(1)}, u32[]{:S(2)}, u32[]{:S(2)}) %collective-permute-start.9) | collective-permute-done | bytes 262176 | tf_op jit(solution)/shard_map/ppermute | solution.py:203
  95.2 3.7 %convert_bitcast_fusion = (bf16[1,1,384,2048]{3,2,1,0:T(8,128)(2,1)}, bf16[384,2048]{1,0:T(8,128)(2,1)S(1)}) fusion(bf16[1,1,384,2048]{3,2,1,0:T(8,128)(2,1)S(1)} %copy-done, bf16[1024,384]{1,0:T(8,128)(2,1)S(1)} %get-tuple-element.164, bf16[1024,2048]{1,0:T(8,128)(2,1)S(1)} %constant_dynamic-update-slice_fusion.10, bf16[1,1,384,2048]{3,2,1,0:T(8,128)(2,1)S(1)} %copy-done.5), kind=kOutput, calls=%fused_computation.72 | convolution fusion | flops 1617690624 | bytes 11272192 | tf_op jit(solution)/shard_map/dot_general | solution.py:368
  104.1 2.4 %bitcast_add_fusion.1 = f32[2048,384]{1,0:T(8,128)S(1)} fusion(bf16[1,1,2048,384]{3,2,1,0:T(8,128)(2,1)S(1)} %copy-done.6, bf16[1024,2048]{1,0:T(8,128)(2,1)S(1)} %get-tuple-element.180, bf16[1024,384]{1,0:T(8,128)(2,1)S(1)} %get-tuple-element.77), kind=kOutput, calls=%fused_computation.5 | convolution fusion | flops 1613758464 | bytes 9699328 | tf_op jit(solution)/shard_map/dot_general | solution.py:391
  106.6 5.1 %convert_bitcast_fusion.1 = (bf16[1,1,2048,384]{3,2,1,0:T(8,128)(2,1)}, bf16[2048,384]{1,0:T(8,128)(2,1)S(1)}, bf16[2048,384]{1,0:T(8,128)(2,1)S(1)}, bf16[1,1,2048,384]{3,2,1,0:T(8,128)(2,1)}) fusion(bf16[1,1,2048,384]{3,2,1,0:T(8,128)(2,1)S(1)} %copy-done.8, f32[2048,384]{1,0:T(8,128)S(1)} %bitcast_add_fusion.1, ...), kind=kOutput, calls=%fused_computation.73 | convolution fusion | flops 1621622784 | bytes 19136512 | tf_op jit(solution)/shard_map/dot_general | solution.py:395
  121.8 2.1 %collective-permute-start.22 = (bf16[256,2048]{1,0:T(8,128)(2,1)S(1)}, bf16[256,2048]{1,0:T(8,128)(2,1)S(1)}, u32[]{:S(2)}, u32[]{:S(2)}) collective-permute-start(bf16[256,2048]{1,0:T(8,128)(2,1)S(1)} %pad_maximum_fusion.2), channel_id=1, source_target_pairs={{0,2},{2,4},{4,6},{6,7},{7,5},{5,3},{3,1},{1,0},{8,10},{10,12},{12... | collective-permute-start | bytes 3145736 | tf_op jit(solution)/shard_map/ppermute | solution.py:203
  126.6 9.5 %collective-permute-done.24 = bf16[384,2048]{1,0:T(8,128)(2,1)S(1)} collective-permute-done((bf16[384,2048]{1,0:T(8,128)(2,1)S(1)}, bf16[384,2048]{1,0:T(8,128)(2,1)S(1)}, u32[]{:S(2)}, u32[]{:S(2)}) %collective-permute-start.24) | collective-permute-done | bytes 1572896 | tf_op jit(solution)/shard_map/ppermute | solution.py:13
  137.4 7.3 %collective-permute-done.23 = bf16[256,2048]{1,0:T(8,128)(2,1)S(1)} collective-permute-done((bf16[256,2048]{1,0:T(8,128)(2,1)S(1)}, bf16[256,2048]{1,0:T(8,128)(2,1)S(1)}, u32[]{:S(2)}, u32[]{:S(2)}) %collective-permute-start.23) | collective-permute-done | bytes 1048608 | tf_op jit(solution)/shard_map/ppermute | solution.py:203
  151.5 19.0 %collective-permute-done.26 = bf16[256,2048]{1,0:T(8,128)(2,1)S(1)} collective-permute-done((bf16[256,2048]{1,0:T(8,128)(2,1)S(1)}, bf16[256,2048]{1,0:T(8,128)(2,1)S(1)}, u32[]{:S(2)}, u32[]{:S(2)}) %collective-permute-start.26) | collective-permute-done | bytes 1048608 | tf_op jit(solution)/shard_map/ppermute | solution.py:203
  174.8 19.1 %collective-permute-done.27 = bf16[256,2048]{1,0:T(8,128)(2,1)S(1)} collective-permute-done((bf16[256,2048]{1,0:T(8,128)(2,1)S(1)}, bf16[256,2048]{1,0:T(8,128)(2,1)S(1)}, u32[]{:S(2)}, u32[]{:S(2)}) %collective-permute-start.27) | collective-permute-done | bytes 1048608 | tf_op jit(solution)/shard_map/ppermute | solution.py:203
  197.0 6.1 %collective-permute-done.30 = bf16[4096,384]{1,0:T(8,128)(2,1)S(1)} collective-permute-done((bf16[4096,384]{1,0:T(8,128)(2,1)S(1)}, bf16[4096,384]{1,0:T(8,128)(2,1)S(1)}, u32[]{:S(2)}, u32[]{:S(2)}) %collective-permute-start.30) | collective-permute-done | bytes 3145760 | tf_op jit(solution)/shard_map/ppermute | solution.py:13
  203.1 2.8 %fusion.12 = (bf16[1,1,2048,384]{3,2,1,0:T(8,128)(2,1)}, bf16[1,1,2048,384]{3,2,1,0:T(8,128)(2,1)}) fusion(bf16[4096,384]{1,0:T(8,128)(2,1)S(1)} %collective-permute-done.30, bf16[4096,384]{1,0:T(8,128)(2,1)S(1)} %fusion, pred[]{:T(512)S(6)} %eq.63), kind=kLoop, calls=%fused_computation.46 | loop fusion | flops 9437184 | bytes 9437185 | tf_op jit(solution)/shard_map/broadcast_in_dim | solution.py:433
  (143 shorter events, 56.5 us)
Async XLA Ops:
  0.6 16.1 %collective-permute-start.1 = (bf16[128,2048]{1,0:T(8,128)(2,1)}, bf16[128,2048]{1,0:T(8,128)(2,1)S(1)}, u32[]{:S(2)}, u32[]{:S(2)}) collective-permute-start(bf16[128,2048]{1,0:T(8,128)(2,1)} %param.12), channel_id=1, source_target_pairs={{0,2},{2,4},{4,6},{6,7},{7,5},{5,3},{3,1},{1,0},{8,10},{10,12},{12... | collective-permute-start | bytes 1572872 | tf_op jit(solution)/shard_map/ppermute | solution.py:203
  3.7 15.1 %collective-permute-start.2 = (bf16[128,2048]{1,0:T(8,128)(2,1)}, bf16[128,2048]{1,0:T(8,128)(2,1)S(1)}, u32[]{:S(2)}, u32[]{:S(2)}) collective-permute-start(bf16[128,2048]{1,0:T(8,128)(2,1)} %param.12), channel_id=1, source_target_pairs={{0,1},{2,0},{4,2},{6,4},{7,6},{5,7},{3,5},{1,3},{8,9},{10,8},{12,1... | collective-permute-start | bytes 1572872 | tf_op jit(solution)/shard_map/ppermute | solution.py:203
  3.7 26.9 %collective-permute-start.11 = (bf16[128,2048]{1,0:T(8,128)(2,1)}, bf16[128,2048]{1,0:T(8,128)(2,1)S(1)}, u32[]{:S(2)}, u32[]{:S(2)}) collective-permute-start(bf16[128,2048]{1,0:T(8,128)(2,1)} %param.15), channel_id=1, source_target_pairs={{0,2},{2,4},{4,6},{6,7},{7,5},{5,3},{3,1},{1,0},{8,10},{10,12},{12... | collective-permute-start | bytes 1572872 | tf_op jit(solution)/shard_map/ppermute | solution.py:203
  5.7 24.9 %collective-permute-start.12 = (bf16[128,2048]{1,0:T(8,128)(2,1)}, bf16[128,2048]{1,0:T(8,128)(2,1)S(1)}, u32[]{:S(2)}, u32[]{:S(2)}) collective-permute-start(bf16[128,2048]{1,0:T(8,128)(2,1)} %param.15), channel_id=1, source_target_pairs={{0,1},{2,0},{4,2},{6,4},{7,6},{5,7},{3,5},{1,3},{8,9},{10,8},{12,1... | collective-permute-start | bytes 1572872 | tf_op jit(solution)/shard_map/ppermute | solution.py:203
  7.8 20.1 %collective-permute-start = (f32[1,8,128]{2,1,0:T(8,128)S(1)}, f32[1,8,128]{2,1,0:T(8,128)S(1)}, u32[]{:S(2)}, u32[]{:S(2)}) collective-permute-start(f32[1,8,128]{2,1,0:T(8,128)S(1)} %bitcast.172), channel_id=1, source_target_pairs={{0,1},{1,0},{2,3},{3,2},{4,5},{5,4},{6,7},{7,6},{8,9},{9,8},{10,11... | collective-permute-start | bytes 12296 | tf_op jit(solution)/shard_map/ppermute | solution.py:223
  18.8 20.4 %collective-permute-start.4 = (bf16[128,2048]{1,0:T(8,128)(2,1)S(1)}, bf16[128,2048]{1,0:T(8,128)(2,1)S(1)}, u32[]{:S(2)}, u32[]{:S(2)}) collective-permute-start(bf16[128,2048]{1,0:T(8,128)(2,1)S(1)} %collective-permute-done.1), channel_id=1, source_target_pairs={{0,2},{2,4},{4,6},{6,7},{7,5},{5,3},{3,1},{1,0},{8,10},{10,12},{12... | collective-permute-start | bytes 1572872 | tf_op jit(solution)/shard_map/ppermute | solution.py:203
  20.3 20.9 %collective-permute-start.5 = (bf16[128,2048]{1,0:T(8,128)(2,1)S(1)}, bf16[128,2048]{1,0:T(8,128)(2,1)S(1)}, u32[]{:S(2)}, u32[]{:S(2)}) collective-permute-start(bf16[128,2048]{1,0:T(8,128)(2,1)S(1)} %collective-permute-done.2), channel_id=1, source_target_pairs={{0,1},{2,0},{4,2},{6,4},{7,6},{5,7},{3,5},{1,3},{8,9},{10,8},{12,1... | collective-permute-start | bytes 1572872 | tf_op jit(solution)/shard_map/ppermute | solution.py:203
  27.9 15.3 %collective-permute-start.3 = (f32[2,8,128]{2,1,0:T(8,128)S(1)}, f32[2,8,128]{2,1,0:T(8,128)S(1)}, u32[]{:S(2)}, u32[]{:S(2)}) collective-permute-start(f32[2,8,128]{2,1,0:T(8,128)S(1)} %pad_maximum_fusion.14), channel_id=1, source_target_pairs={{0,2},{1,3},{2,0},{3,1},{4,6},{5,7},{6,4},{7,5},{8,10},{9,11},{10,... | collective-permute-start | bytes 24584 | tf_op jit(solution)/shard_map/ppermute | solution.py:223
  30.6 19.8 %collective-permute-start.13 = (bf16[128,2048]{1,0:T(8,128)(2,1)S(1)}, bf16[128,2048]{1,0:T(8,128)(2,1)S(1)}, u32[]{:S(2)}, u32[]{:S(2)}) collective-permute-start(bf16[128,2048]{1,0:T(8,128)(2,1)S(1)} %collective-permute-done.11), channel_id=1, source_target_pairs={{0,2},{2,4},{4,6},{6,7},{7,5},{5,3},{3,1},{1,0},{8,10},{10,12},{12... | collective-permute-start | bytes 1572872 | tf_op jit(solution)/shard_map/ppermute | solution.py:203
  32.5 20.1 %collective-permute-start.14 = (bf16[128,2048]{1,0:T(8,128)(2,1)S(1)}, bf16[128,2048]{1,0:T(8,128)(2,1)S(1)}, u32[]{:S(2)}, u32[]{:S(2)}) collective-permute-start(bf16[128,2048]{1,0:T(8,128)(2,1)S(1)} %collective-permute-done.12), channel_id=1, source_target_pairs={{0,1},{2,0},{4,2},{6,4},{7,6},{5,7},{3,5},{1,3},{8,9},{10,8},{12,1... | collective-permute-start | bytes 1572872 | tf_op jit(solution)/shard_map/ppermute | solution.py:203
  41.2 20.4 %collective-permute-start.7 = (bf16[128,2048]{1,0:T(8,128)(2,1)S(1)}, bf16[128,2048]{1,0:T(8,128)(2,1)S(1)}, u32[]{:S(2)}, u32[]{:S(2)}) collective-permute-start(bf16[128,2048]{1,0:T(8,128)(2,1)S(1)} %collective-permute-done.4), channel_id=1, source_target_pairs={{0,2},{2,4},{4,6},{6,7},{7,5},{5,3},{3,1},{1,0},{8,10},{10,12},{12... | collective-permute-start | bytes 1572872 | tf_op jit(solution)/shard_map/ppermute | solution.py:203
  42.8 21.2 %collective-permute-start.8 = (bf16[128,2048]{1,0:T(8,128)(2,1)S(1)}, bf16[128,2048]{1,0:T(8,128)(2,1)S(1)}, u32[]{:S(2)}, u32[]{:S(2)}) collective-permute-start(bf16[128,2048]{1,0:T(8,128)(2,1)S(1)} %collective-permute-done.5), channel_id=1, source_target_pairs={{0,1},{2,0},{4,2},{6,4},{7,6},{5,7},{3,5},{1,3},{8,9},{10,8},{12,1... | collective-permute-start | bytes 1572872 | tf_op jit(solution)/shard_map/ppermute | solution.py:203
  43.3 22.0 %collective-permute-start.6 = (f32[4,8,128]{2,1,0:T(8,128)S(1)}, f32[4,8,128]{2,1,0:T(8,128)S(1)}, u32[]{:S(2)}, u32[]{:S(2)}) collective-permute-start(f32[4,8,128]{2,1,0:T(8,128)S(1)} %pad_maximum_fusion.13), channel_id=1, source_target_pairs={{0,4},{1,5},{2,6},{3,7},{4,0},{5,1},{6,2},{7,3},{8,12},{9,13},{10,... | collective-permute-start | bytes 49160 | tf_op jit(solution)/shard_map/ppermute | solution.py:223
  52.6 21.4 %collective-permute-start.16 = (bf16[128,2048]{1,0:T(8,128)(2,1)S(1)}, bf16[128,2048]{1,0:T(8,128)(2,1)S(1)}, u32[]{:S(2)}, u32[]{:S(2)}) collective-permute-start(bf16[128,2048]{1,0:T(8,128)(2,1)S(1)} %collective-permute-done.14), channel_id=1, source_target_pairs={{0,1},{2,0},{4,2},{6,4},{7,6},{5,7},{3,5},{1,3},{8,9},{10,8},{12,1... | collective-permute-start | bytes 1572872 | tf_op jit(solution)/shard_map/ppermute | solution.py:203
  52.7 19.4 %collective-permute-start.15 = (bf16[128,2048]{1,0:T(8,128)(2,1)S(1)}, bf16[128,2048]{1,0:T(8,128)(2,1)S(1)}, u32[]{:S(2)}, u32[]{:S(2)}) collective-permute-start(bf16[128,2048]{1,0:T(8,128)(2,1)S(1)} %collective-permute-done.13), channel_id=1, source_target_pairs={{0,2},{2,4},{4,6},{6,7},{7,5},{5,3},{3,1},{1,0},{8,10},{10,12},{12... | collective-permute-start | bytes 1572872 | tf_op jit(solution)/shard_map/ppermute | solution.py:203
  74.1 14.4 %copy-start = (bf16[1,1,384,2048]{3,2,1,0:T(8,128)(2,1)S(1)}, bf16[1,1,384,2048]{3,2,1,0:T(8,128)(2,1)}, u32[]{:S(2)}) copy-start(bf16[1,1,384,2048]{3,2,1,0:T(8,128)(2,1)} %param.18) | copy-start | bytes 4718596
  74.2 19.0 %collective-permute-start.17 = (bf16[64,2048]{1,0:T(8,128)(2,1)S(1)}, bf16[64,2048]{1,0:T(8,128)(2,1)S(1)}, u32[]{:S(2)}, u32[]{:S(2)}) collective-permute-start(bf16[64,2048]{1,0:T(8,128)(2,1)S(1)} %slice.128), channel_id=1, source_target_pairs={{0,2},{2,4},{4,6},{6,7},{7,5},{5,3},{3,1},{1,0},{8,10},{10,12},{12... | collective-permute-start | bytes 786440 | tf_op jit(solution)/shard_map/ppermute | solution.py:203
  76.0 17.8 %collective-permute-start.18 = (bf16[64,2048]{1,0:T(8,128)(2,1)S(1)}, bf16[64,2048]{1,0:T(8,128)(2,1)S(1)}, u32[]{:S(2)}, u32[]{:S(2)}) collective-permute-start(bf16[64,2048]{1,0:T(8,128)(2,1)S(1)} %slice.129), channel_id=1, source_target_pairs={{0,1},{2,0},{4,2},{6,4},{7,6},{5,7},{3,5},{1,3},{8,9},{10,8},{12,1... | collective-permute-start | bytes 786440 | tf_op jit(solution)/shard_map/ppermute | solution.py:203
  76.3 10.4 %collective-permute-start.9 = (bf16[64,2048]{1,0:T(8,128)(2,1)S(1)}, bf16[64,2048]{1,0:T(8,128)(2,1)S(1)}, u32[]{:S(2)}, u32[]{:S(2)}) collective-permute-start(bf16[64,2048]{1,0:T(8,128)(2,1)S(1)} %slice.104), channel_id=1, source_target_pairs={{0,2},{2,4},{4,6},{6,7},{7,5},{5,3},{3,1},{1,0},{8,10},{10,12},{12... | collective-permute-start | bytes 786440 | tf_op jit(solution)/shard_map/ppermute | solution.py:203
  78.1 10.1 %collective-permute-start.10 = (bf16[64,2048]{1,0:T(8,128)(2,1)S(1)}, bf16[64,2048]{1,0:T(8,128)(2,1)S(1)}, u32[]{:S(2)}, u32[]{:S(2)}) collective-permute-start(bf16[64,2048]{1,0:T(8,128)(2,1)S(1)} %slice.105), channel_id=1, source_target_pairs={{0,1},{2,0},{4,2},{6,4},{7,6},{5,7},{3,5},{1,3},{8,9},{10,8},{12,1... | collective-permute-start | bytes 786440 | tf_op jit(solution)/shard_map/ppermute | solution.py:203
  98.9 21.3 %collective-permute-start.21 = (bf16[384,2048]{1,0:T(8,128)(2,1)S(1)}, bf16[384,2048]{1,0:T(8,128)(2,1)S(1)}, u32[]{:S(2)}, u32[]{:S(2)}) collective-permute-start(bf16[384,2048]{1,0:T(8,128)(2,1)S(1)} %get-tuple-element.141), channel_id=1, source_target_pairs={{0,8},{8,0},{16,24},{24,16},{1,9},{9,1},{17,25},{25,17},{2,10},{10... | collective-permute-start | bytes 4718600 | tf_op jit(solution)/shard_map/ppermute | solution.py:13
  98.9 37.2 %collective-permute-start.24 = (bf16[384,2048]{1,0:T(8,128)(2,1)S(1)}, bf16[384,2048]{1,0:T(8,128)(2,1)S(1)}, u32[]{:S(2)}, u32[]{:S(2)}) collective-permute-start(bf16[384,2048]{1,0:T(8,128)(2,1)S(1)} %get-tuple-element.141), channel_id=1, source_target_pairs={{0,16},{8,24},{16,0},{24,8},{1,17},{9,25},{17,1},{25,9},{2,18},{10... | collective-permute-start | bytes 4718600 | tf_op jit(solution)/shard_map/ppermute | solution.py:13
  102.0 17.7 %collective-permute-start.20 = (bf16[128,2048]{1,0:T(8,128)(2,1)S(1)}, bf16[128,2048]{1,0:T(8,128)(2,1)S(1)}, u32[]{:S(2)}, u32[]{:S(2)}) collective-permute-start(bf16[128,2048]{1,0:T(8,128)(2,1)S(1)} %convolution_multiply_fusion.14), channel_id=1, source_target_pairs={{0,1},{2,0},{4,2},{6,4},{7,6},{5,7},{3,5},{1,3},{8,9},{10,8},{12,1... | collective-permute-start | bytes 1572872 | tf_op jit(solution)/shard_map/ppermute | solution.py:203
  102.3 17.6 %collective-permute-start.19 = (bf16[128,2048]{1,0:T(8,128)(2,1)S(1)}, bf16[128,2048]{1,0:T(8,128)(2,1)S(1)}, u32[]{:S(2)}, u32[]{:S(2)}) collective-permute-start(bf16[128,2048]{1,0:T(8,128)(2,1)S(1)} %convolution_multiply_fusion.15), channel_id=1, source_target_pairs={{0,2},{2,4},{4,6},{6,7},{7,5},{5,3},{3,1},{1,0},{8,10},{10,12},{12... | collective-permute-start | bytes 1572872 | tf_op jit(solution)/shard_map/ppermute | solution.py:203
  112.0 91.1 %collective-permute-start.30 = (bf16[4096,384]{1,0:T(8,128)(2,1)S(1)}, bf16[4096,384]{1,0:T(8,128)(2,1)S(1)}, u32[]{:S(2)}, u32[]{:S(2)}) collective-permute-start(bf16[4096,384]{1,0:T(8,128)(2,1)S(1)} %pad_maximum_fusion.1), channel_id=1, source_target_pairs={{0,16},{8,24},{16,0},{24,8},{1,17},{9,25},{17,1},{25,9},{2,18},{10... | collective-permute-start | bytes 9437192 | tf_op jit(solution)/shard_map/ppermute | solution.py:13
  120.2 24.5 %collective-permute-start.23 = (bf16[256,2048]{1,0:T(8,128)(2,1)S(1)}, bf16[256,2048]{1,0:T(8,128)(2,1)S(1)}, u32[]{:S(2)}, u32[]{:S(2)}) collective-permute-start(bf16[256,2048]{1,0:T(8,128)(2,1)S(1)} %pad_maximum_fusion.3), channel_id=1, source_target_pairs={{0,1},{2,0},{4,2},{6,4},{7,6},{5,7},{3,5},{1,3},{8,9},{10,8},{12,1... | collective-permute-start | bytes 3145736 | tf_op jit(solution)/shard_map/ppermute | solution.py:203
  121.8 24.8 %collective-permute-start.22 = (bf16[256,2048]{1,0:T(8,128)(2,1)S(1)}, bf16[256,2048]{1,0:T(8,128)(2,1)S(1)}, u32[]{:S(2)}, u32[]{:S(2)}) collective-permute-start(bf16[256,2048]{1,0:T(8,128)(2,1)S(1)} %pad_maximum_fusion.2), channel_id=1, source_target_pairs={{0,2},{2,4},{4,6},{6,7},{7,5},{5,3},{3,1},{1,0},{8,10},{10,12},{12... | collective-permute-start | bytes 3145736 | tf_op jit(solution)/shard_map/ppermute | solution.py:203
  136.1 37.6 %collective-permute-start.29 = (bf16[4096,384]{1,0:T(8,128)(2,1)S(1)}, bf16[4096,384]{1,0:T(8,128)(2,1)S(1)}, u32[]{:S(2)}, u32[]{:S(2)}) collective-permute-start(bf16[4096,384]{1,0:T(8,128)(2,1)S(1)} %pad_maximum_fusion.1), channel_id=1, source_target_pairs={{0,8},{8,0},{16,24},{24,16},{1,9},{9,1},{17,25},{25,17},{2,10},{10... | collective-permute-start | bytes 9437192 | tf_op jit(solution)/shard_map/ppermute | solution.py:13
  146.9 23.6 %collective-permute-start.26 = (bf16[256,2048]{1,0:T(8,128)(2,1)S(1)}, bf16[256,2048]{1,0:T(8,128)(2,1)S(1)}, u32[]{:S(2)}, u32[]{:S(2)}) collective-permute-start(bf16[256,2048]{1,0:T(8,128)(2,1)S(1)} %fusion.9), channel_id=1, source_target_pairs={{0,1},{2,0},{4,2},{6,4},{7,6},{5,7},{3,5},{1,3},{8,9},{10,8},{12,1... | collective-permute-start | bytes 3145736 | tf_op jit(solution)/shard_map/ppermute | solution.py:203
  148.0 23.3 %collective-permute-start.25 = (bf16[256,2048]{1,0:T(8,128)(2,1)S(1)}, bf16[256,2048]{1,0:T(8,128)(2,1)S(1)}, u32[]{:S(2)}, u32[]{:S(2)}) collective-permute-start(bf16[256,2048]{1,0:T(8,128)(2,1)S(1)} %fusion.8), channel_id=1, source_target_pairs={{0,2},{2,4},{4,6},{6,7},{7,5},{5,3},{3,1},{1,0},{8,10},{10,12},{12... | collective-permute-start | bytes 3145736 | tf_op jit(solution)/shard_map/ppermute | solution.py:203
  171.6 22.4 %collective-permute-start.27 = (bf16[256,2048]{1,0:T(8,128)(2,1)S(1)}, bf16[256,2048]{1,0:T(8,128)(2,1)S(1)}, u32[]{:S(2)}, u32[]{:S(2)}) collective-permute-start(bf16[256,2048]{1,0:T(8,128)(2,1)S(1)} %fusion.7), channel_id=1, source_target_pairs={{0,2},{2,4},{4,6},{6,7},{7,5},{5,3},{3,1},{1,0},{8,10},{10,12},{12... | collective-permute-start | bytes 3145736 | tf_op jit(solution)/shard_map/ppermute | solution.py:203
  173.4 22.1 %collective-permute-start.28 = (bf16[256,2048]{1,0:T(8,128)(2,1)S(1)}, bf16[256,2048]{1,0:T(8,128)(2,1)S(1)}, u32[]{:S(2)}, u32[]{:S(2)}) collective-permute-start(bf16[256,2048]{1,0:T(8,128)(2,1)S(1)} %fusion.10), channel_id=1, source_target_pairs={{0,1},{2,0},{4,2},{6,4},{7,6},{5,7},{3,5},{1,3},{8,9},{10,8},{12,1... | collective-permute-start | bytes 3145736 | tf_op jit(solution)/shard_map/ppermute | solution.py:203
  (9 other events, 59.8 us)
where the time goes:
time: 206 us
  waiting for transfers between devices  112 us (54%)
  matrix products  41.2 us (20%)
  starting transfers between devices  33.2 us (16%)
  other arithmetic  11.4 us (6%)
  local copies, waits for them, and re-layouts  5.85 us (3%)
  between operations  2.07 us (1%)
    ppermute x24, waiting for transfers between devices, ring_hop(): return lax.ppermute(value, 'expert', pairs)  88.2 us
    ppermute x24, starting transfers between devices, ring_hop(): return lax.ppermute(value, 'expert', pairs)  26.5 us
    ppermute x4, waiting for transfers between devices, partner_2(): return lax.ppermute(value, axis, pairs)  15.6 us
    dot_general x8, matrix products, per_device_dense(): jnp.dot(block, weight_both, preferred_element_type=jnp.float32) * scale_in  11 us
    dot_general x8, matrix products, parts_of(): lax.dot_general(both_grad, weight_both, inner_dims, preferred_element_typ...  10.2 us
    ppermute x3, waiting for transfers between devices, ring_gather_pair(): swapped = lax.ppermute(table, 'expert', pairs)  8.31 us
    dot_general x8, matrix products, per_device_dense(): lax.dot_general(cot, weight_down, inner_dims, preferred_element_type=jnp....  5.29 us
    dot_general x1, matrix products, per_device_dense(): lax.dot_general(rows_in, grad_up_pre, outer_dims, preferred_element_type=...  5.08 us
  transfers between devices with their start and end apart: 31, of which 21 were waited for; matrix products, arithmetic and copies ran while one was open for 24% of the time, Pallas kernels for 0%

commit v1 on v0

--- a/solution.py
+++ b/solution.py
@@ -208,7 +208,6 @@
 
 
 def ring_gather_pair(first, second, table, experts):
-    half = first.shape[0] // 2
     last = experts // 2
     blocks = [[None] * experts, [None] * experts]
     moving = [(first, first), (second, second)]
@@ -232,11 +231,8 @@
             else:
                 moving[1] = after((behind, ahead), moving[0], table)
             blocks[which][experts - step], blocks[which][step] = moving[which]
-    for which in range(2):
-        behind, ahead = moving[which]
-        top = ring_hop(behind[:half], experts, 1)
-        bottom = ring_hop(ahead[half:], experts, -1)
-        blocks[which][last] = jnp.concatenate([top, bottom], axis=0)
+    blocks[0][last] = ring_hop(moving[0][0], experts, 1)
+    blocks[1][last] = ring_hop(moving[1][1], experts, -1)
     while table.shape[0] < experts:
         bit = table.shape[0]
         pairs = [(e, e ^ bit) for e in range(experts)]
@@ -310,7 +306,7 @@
     table = share_table(routing, gate_share, experts)
     blocks, tables = ring_gather_pair(tokens, cotangent, table, experts)
     tok_blocks, cot_blocks = blocks
-    share_blocks = own_shares(after(tables, tok_blocks[experts // 2]), experts)
+    share_blocks = own_shares(tables, experts)
     weight_both = jnp.concatenate([weight_gate, weight_up], axis=1)
 
     arrival = [0]

time: 206 us -> 198 us (0.961)
  waiting for transfers between devices: 112 us -> 106 us
    ppermute x24 -> x22, waiting for transfers between devices: 88.2 us -> 84.1 us  [ring_hop(): return lax.ppermute(value, 'expert', pairs)]
    ppermute x24 -> x22, starting transfers between devices: 26.5 us -> 25 us  [ring_hop(): return lax.ppermute(value, 'expert', pairs)]
  transfers between devices with their start and end apart: 31 -> 29, of which waited for: 21 -> 20; matrix products, arithmetic and copies ran while one was open for 24% -> 26% of each run, Pallas kernels for 0% -> 0%
where the time goes in v1:
time: 198 us
  waiting for transfers between devices  106 us (54%)
  matrix products  41.4 us (21%)
  starting transfers between devices  31.7 us (16%)
  other arithmetic  11.4 us (6%)
  local copies, waits for them, and re-layouts  5.57 us (3%)
  between operations  2.03 us (1%)
    ppermute x22, waiting for transfers between devices, ring_hop(): return lax.ppermute(value, 'expert', pairs)  84.1 us
    ppermute x22, starting transfers between devices, ring_hop(): return lax.ppermute(value, 'expert', pairs)  25 us
    ppermute x4, waiting for transfers between devices, partner_2(): return lax.ppermute(value, axis, pairs)  14.6 us
    dot_general x8, matrix products, per_device_dense(): jnp.dot(block, weight_both, preferred_element_type=jnp.float32) * scale_in  11 us
    dot_general x8, matrix products, parts_of(): lax.dot_general(both_grad, weight_both, inner_dims, preferred_element_typ...  10.3 us
    ppermute x3, waiting for transfers between devices, ring_gather_pair(): swapped = lax.ppermute(table, 'expert', pairs)  7.15 us
    dot_general x8, matrix products, per_device_dense(): lax.dot_general(cot, weight_down, inner_dims, preferred_element_type=jnp....  5.29 us
    dot_general x1, matrix products, per_device_dense(): lax.dot_general(rows_in, grad_up_pre, outer_dims, preferred_element_type=...  5.11 us
  transfers between devices with their start and end apart: 29, of which 20 were waited for; matrix products, arithmetic and copies ran while one was open for 26% of the time, Pallas kernels for 0%

profile of v1, /device:TPU:0, one launch (start us, length us, event | category | flops | bytes accessed | tf_op | source)
XLA Modules:
  0.0 198.0 jit_solution(10526151396865764661)
XLA Ops:
  0.6 3.1 %collective-permute-start.1 = (bf16[128,2048]{1,0:T(8,128)(2,1)}, bf16[128,2048]{1,0:T(8,128)(2,1)S(1)}, u32[]{:S(2)}, u32[]{:S(2)}) collective-permute-start(bf16[128,2048]{1,0:T(8,128)(2,1)} %param.12), channel_id=1, source_target_pairs={{0,2},{2,4},{4,6},{6,7},{7,5},{5,3},{3,1},{1,0},{8,10},{10,12},{12... | collective-permute-start | bytes 1572872 | tf_op jit(solution)/shard_map/ppermute | solution.py:203
  3.7 2.0 %collective-permute-start.10 = (bf16[128,2048]{1,0:T(8,128)(2,1)}, bf16[128,2048]{1,0:T(8,128)(2,1)S(1)}, u32[]{:S(2)}, u32[]{:S(2)}) collective-permute-start(bf16[128,2048]{1,0:T(8,128)(2,1)} %param.15), channel_id=1, source_target_pairs={{0,2},{2,4},{4,6},{6,7},{7,5},{5,3},{3,1},{1,0},{8,10},{10,12},{12... | collective-permute-start | bytes 1572872 | tf_op jit(solution)/shard_map/ppermute | solution.py:203
  7.8 2.0 %collective-permute-start = (f32[1,8,128]{2,1,0:T(8,128)S(1)}, f32[1,8,128]{2,1,0:T(8,128)S(1)}, u32[]{:S(2)}, u32[]{:S(2)}) collective-permute-start(f32[1,8,128]{2,1,0:T(8,128)S(1)} %bitcast.173), channel_id=1, source_target_pairs={{0,1},{1,0},{2,3},{3,2},{4,5},{5,4},{6,7},{7,6},{8,9},{9,8},{10,11... | collective-permute-start | bytes 12296 | tf_op jit(solution)/shard_map/ppermute | solution.py:222
  9.9 1.9 constant_dynamic-update-slice_fusion.15
  12.4 2.7 %fusion.38 = f32[128,768]{1,0:T(8,128)S(1)} fusion(bf16[128,2048]{1,0:T(8,128)(2,1)} %param.12, bf16[2048,384]{1,0:T(8,128)(2,1)} %bitcast.177, bf16[2048,384]{1,0:T(8,128)(2,1)} %bitcast.193), kind=kOutput, calls=%fused_computation.76 | convolution fusion | flops 409042944 | bytes 4063232 | tf_op jit(solution)/shard_map/dot_general | solution.py:320
  16.7 2.0 %collective-permute-done.2 = bf16[128,2048]{1,0:T(8,128)(2,1)S(1)} collective-permute-done((bf16[128,2048]{1,0:T(8,128)(2,1)}, bf16[128,2048]{1,0:T(8,128)(2,1)S(1)}, u32[]{:S(2)}, u32[]{:S(2)}) %collective-permute-start.2) | collective-permute-done | bytes 524320 | tf_op jit(solution)/shard_map/ppermute | solution.py:203
  20.8 7.1 %collective-permute-done = f32[1,8,128]{2,1,0:T(8,128)S(1)} collective-permute-done((f32[1,8,128]{2,1,0:T(8,128)S(1)}, f32[1,8,128]{2,1,0:T(8,128)S(1)}, u32[]{:S(2)}, u32[]{:S(2)}) %collective-permute-start) | collective-permute-done | bytes 4128 | tf_op jit(solution)/shard_map/ppermute | solution.py:222
  28.0 2.6 %convolution_multiply_fusion.23 = f32[128,768]{1,0:T(8,128)S(1)} fusion(bf16[128,2048]{1,0:T(8,128)(2,1)S(1)} %collective-permute-done.2, bf16[2048,384]{1,0:T(8,128)(2,1)} %bitcast.178, bf16[2048,384]{1,0:T(8,128)(2,1)} %bitcast.194), kind=kOutput, calls=%fused_computation.83 | convolution fusion | flops 409042944 | bytes 4063232 | tf_op jit(solution)/shard_map/dot_general | solution.py:320
  30.6 1.9 collective-permute-start.12
  33.0 2.6 %convolution_multiply_fusion.22 = f32[128,768]{1,0:T(8,128)S(1)} fusion(bf16[128,2048]{1,0:T(8,128)(2,1)S(1)} %collective-permute-done.1, bf16[2048,384]{1,0:T(8,128)(2,1)} %bitcast.179, bf16[2048,384]{1,0:T(8,128)(2,1)} %bitcast.195), kind=kOutput, calls=%fused_computation.82 | convolution fusion | flops 409042944 | bytes 4063232 | tf_op jit(solution)/shard_map/dot_general | solution.py:320
  35.7 3.5 %collective-permute-done.4 = bf16[128,2048]{1,0:T(8,128)(2,1)S(1)} collective-permute-done((bf16[128,2048]{1,0:T(8,128)(2,1)S(1)}, bf16[128,2048]{1,0:T(8,128)(2,1)S(1)}, u32[]{:S(2)}, u32[]{:S(2)}) %collective-permute-start.4) | collective-permute-done | bytes 524320 | tf_op jit(solution)/shard_map/ppermute | solution.py:203
  39.2 2.1 %collective-permute-done.5 = bf16[128,2048]{1,0:T(8,128)(2,1)S(1)} collective-permute-done((bf16[128,2048]{1,0:T(8,128)(2,1)S(1)}, bf16[128,2048]{1,0:T(8,128)(2,1)S(1)}, u32[]{:S(2)}, u32[]{:S(2)}) %collective-permute-start.5) | collective-permute-done | bytes 524320 | tf_op jit(solution)/shard_map/ppermute | solution.py:203
  43.3 2.6 %collective-permute-start.6 = (f32[4,8,128]{2,1,0:T(8,128)S(1)}, f32[4,8,128]{2,1,0:T(8,128)S(1)}, u32[]{:S(2)}, u32[]{:S(2)}) collective-permute-start(f32[4,8,128]{2,1,0:T(8,128)S(1)} %pad_maximum_fusion.13), channel_id=1, source_target_pairs={{0,4},{1,5},{2,6},{3,7},{4,0},{5,1},{6,2},{7,3},{8,12},{9,13},{10,... | collective-permute-start | bytes 49160 | tf_op jit(solution)/shard_map/ppermute | solution.py:222
  46.5 3.9 %collective-permute-done.12 = bf16[128,2048]{1,0:T(8,128)(2,1)S(1)} collective-permute-done((bf16[128,2048]{1,0:T(8,128)(2,1)S(1)}, bf16[128,2048]{1,0:T(8,128)(2,1)S(1)}, u32[]{:S(2)}, u32[]{:S(2)}) %collective-permute-start.12) | collective-permute-done | bytes 524320 | tf_op jit(solution)/shard_map/ppermute | solution.py:203
  50.4 2.2 %collective-permute-done.13 = bf16[128,2048]{1,0:T(8,128)(2,1)S(1)} collective-permute-done((bf16[128,2048]{1,0:T(8,128)(2,1)S(1)}, bf16[128,2048]{1,0:T(8,128)(2,1)S(1)}, u32[]{:S(2)}, u32[]{:S(2)}) %collective-permute-start.13) | collective-permute-done | bytes 524320 | tf_op jit(solution)/shard_map/ppermute | solution.py:203
  52.7 2.1 %collective-permute-start.14 = (bf16[128,2048]{1,0:T(8,128)(2,1)S(1)}, bf16[128,2048]{1,0:T(8,128)(2,1)S(1)}, u32[]{:S(2)}, u32[]{:S(2)}) collective-permute-start(bf16[128,2048]{1,0:T(8,128)(2,1)S(1)} %collective-permute-done.12), channel_id=1, source_target_pairs={{0,2},{2,4},{4,6},{6,7},{7,5},{5,3},{3,1},{1,0},{8,10},{10,12},{12... | collective-permute-start | bytes 1572872 | tf_op jit(solution)/shard_map/ppermute | solution.py:203
  55.5 6.1 %collective-permute-done.7 = bf16[128,2048]{1,0:T(8,128)(2,1)S(1)} collective-permute-done((bf16[128,2048]{1,0:T(8,128)(2,1)S(1)}, bf16[128,2048]{1,0:T(8,128)(2,1)S(1)}, u32[]{:S(2)}, u32[]{:S(2)}) %collective-permute-start.7) | collective-permute-done | bytes 524320 | tf_op jit(solution)/shard_map/ppermute | solution.py:203
  61.6 2.4 %collective-permute-done.8 = bf16[128,2048]{1,0:T(8,128)(2,1)S(1)} collective-permute-done((bf16[128,2048]{1,0:T(8,128)(2,1)S(1)}, bf16[128,2048]{1,0:T(8,128)(2,1)S(1)}, u32[]{:S(2)}, u32[]{:S(2)}) %collective-permute-start.8) | collective-permute-done | bytes 524320 | tf_op jit(solution)/shard_map/ppermute | solution.py:203
  67.0 6.0 %collective-permute-done.14 = bf16[128,2048]{1,0:T(8,128)(2,1)S(1)} collective-permute-done((bf16[128,2048]{1,0:T(8,128)(2,1)S(1)}, bf16[128,2048]{1,0:T(8,128)(2,1)S(1)}, u32[]{:S(2)}, u32[]{:S(2)}) %collective-permute-start.14) | collective-permute-done | bytes 524320 | tf_op jit(solution)/shard_map/ppermute | solution.py:203
  80.4 2.8 %collective-permute-done.9 = bf16[128,2048]{1,0:T(8,128)(2,1)S(1)} collective-permute-done((bf16[128,2048]{1,0:T(8,128)(2,1)S(1)}, bf16[128,2048]{1,0:T(8,128)(2,1)S(1)}, u32[]{:S(2)}, u32[]{:S(2)}) %collective-permute-start.9) | collective-permute-done | bytes 524320 | tf_op jit(solution)/shard_map/ppermute | solution.py:203
  83.9 2.6 %collective-permute-done.16 = bf16[128,2048]{1,0:T(8,128)(2,1)S(1)} collective-permute-done((bf16[128,2048]{1,0:T(8,128)(2,1)S(1)}, bf16[128,2048]{1,0:T(8,128)(2,1)S(1)}, u32[]{:S(2)}, u32[]{:S(2)}) %collective-permute-start.16) | collective-permute-done | bytes 524320 | tf_op jit(solution)/shard_map/ppermute | solution.py:203
  87.2 3.7 %convert_bitcast_fusion = (bf16[1,1,384,2048]{3,2,1,0:T(8,128)(2,1)}, bf16[384,2048]{1,0:T(8,128)(2,1)S(1)}) fusion(bf16[1,1,384,2048]{3,2,1,0:T(8,128)(2,1)S(1)} %copy-done, bf16[1024,384]{1,0:T(8,128)(2,1)S(1)} %get-tuple-element.162, bf16[1024,2048]{1,0:T(8,128)(2,1)S(1)} %constant_dynamic-update-slice_fusion.8, bf16[1,1,384,2048]{3,2,1,0:T(8,128)(2,1)S(1)} %copy-done.5), kind=kOutput, calls=%fused_computation.72 | convolution fusion | flops 1617690624 | bytes 11272192 | tf_op jit(solution)/shard_map/dot_general | solution.py:364
  96.2 2.5 %bitcast_add_fusion.1 = f32[2048,384]{1,0:T(8,128)S(1)} fusion(bf16[1,1,2048,384]{3,2,1,0:T(8,128)(2,1)S(1)} %copy-done.6, bf16[1024,2048]{1,0:T(8,128)(2,1)S(1)} %constant_dynamic-update-slice_fusion.16, bf16[1024,384]{1,0:T(8,128)(2,1)S(1)} %get-tuple-element.75), kind=kOutput, calls=%fused_computation.5 | convolution fusion | flops 1613758464 | bytes 9699328 | tf_op jit(solution)/shard_map/dot_general | solution.py:387
  98.7 5.1 %convert_bitcast_fusion.1 = (bf16[1,1,2048,384]{3,2,1,0:T(8,128)(2,1)}, bf16[2048,384]{1,0:T(8,128)(2,1)S(1)}, bf16[2048,384]{1,0:T(8,128)(2,1)S(1)}, bf16[1,1,2048,384]{3,2,1,0:T(8,128)(2,1)}) fusion(bf16[1,1,2048,384]{3,2,1,0:T(8,128)(2,1)S(1)} %copy-done.8, f32[2048,384]{1,0:T(8,128)S(1)} %bitcast_add_fusion.1, ...), kind=kOutput, calls=%fused_computation.73 | convolution fusion | flops 1621622784 | bytes 19136512 | tf_op jit(solution)/shard_map/dot_general | solution.py:391
  114.6 1.8 collective-permute-start.20
  119.1 8.9 %collective-permute-done.22 = bf16[384,2048]{1,0:T(8,128)(2,1)S(1)} collective-permute-done((bf16[384,2048]{1,0:T(8,128)(2,1)S(1)}, bf16[384,2048]{1,0:T(8,128)(2,1)S(1)}, u32[]{:S(2)}, u32[]{:S(2)}) %collective-permute-start.22) | collective-permute-done | bytes 1572896 | tf_op jit(solution)/shard_map/ppermute | solution.py:13
  129.4 8.1 %collective-permute-done.21 = bf16[256,2048]{1,0:T(8,128)(2,1)S(1)} collective-permute-done((bf16[256,2048]{1,0:T(8,128)(2,1)S(1)}, bf16[256,2048]{1,0:T(8,128)(2,1)S(1)}, u32[]{:S(2)}, u32[]{:S(2)}) %collective-permute-start.21) | collective-permute-done | bytes 1048608 | tf_op jit(solution)/shard_map/ppermute | solution.py:203
  142.2 1.8 fusion.11
  144.0 19.1 %collective-permute-done.24 = bf16[256,2048]{1,0:T(8,128)(2,1)S(1)} collective-permute-done((bf16[256,2048]{1,0:T(8,128)(2,1)S(1)}, bf16[256,2048]{1,0:T(8,128)(2,1)S(1)}, u32[]{:S(2)}, u32[]{:S(2)}) %collective-permute-start.24) | collective-permute-done | bytes 1048608 | tf_op jit(solution)/shard_map/ppermute | solution.py:203
  168.5 18.8 %collective-permute-done.25 = bf16[256,2048]{1,0:T(8,128)(2,1)S(1)} collective-permute-done((bf16[256,2048]{1,0:T(8,128)(2,1)S(1)}, bf16[256,2048]{1,0:T(8,128)(2,1)S(1)}, u32[]{:S(2)}, u32[]{:S(2)}) %collective-permute-start.25) | collective-permute-done | bytes 1048608 | tf_op jit(solution)/shard_map/ppermute | solution.py:203
  189.4 5.7 %collective-permute-done.28 = bf16[4096,384]{1,0:T(8,128)(2,1)S(1)} collective-permute-done((bf16[4096,384]{1,0:T(8,128)(2,1)S(1)}, bf16[4096,384]{1,0:T(8,128)(2,1)S(1)}, u32[]{:S(2)}, u32[]{:S(2)}) %collective-permute-start.28) | collective-permute-done | bytes 3145760 | tf_op jit(solution)/shard_map/ppermute | solution.py:13
  195.1 2.9 %fusion.12 = (bf16[1,1,2048,384]{3,2,1,0:T(8,128)(2,1)}, bf16[1,1,2048,384]{3,2,1,0:T(8,128)(2,1)}) fusion(bf16[4096,384]{1,0:T(8,128)(2,1)S(1)} %collective-permute-done.28, bf16[4096,384]{1,0:T(8,128)(2,1)S(1)} %fusion, pred[]{:T(512)S(6)} %eq.63), kind=kLoop, calls=%fused_computation.46 | loop fusion | flops 9437184 | bytes 9437185 | tf_op jit(solution)/shard_map/broadcast_in_dim | solution.py:429
  (136 shorter events, 53.4 us)
Async XLA Ops:
  0.6 16.1 %collective-permute-start.1 = (bf16[128,2048]{1,0:T(8,128)(2,1)}, bf16[128,2048]{1,0:T(8,128)(2,1)S(1)}, u32[]{:S(2)}, u32[]{:S(2)}) collective-permute-start(bf16[128,2048]{1,0:T(8,128)(2,1)} %param.12), channel_id=1, source_target_pairs={{0,2},{2,4},{4,6},{6,7},{7,5},{5,3},{3,1},{1,0},{8,10},{10,12},{12... | collective-permute-start | bytes 1572872 | tf_op jit(solution)/shard_map/ppermute | solution.py:203
  3.7 15.1 %collective-permute-start.2 = (bf16[128,2048]{1,0:T(8,128)(2,1)}, bf16[128,2048]{1,0:T(8,128)(2,1)S(1)}, u32[]{:S(2)}, u32[]{:S(2)}) collective-permute-start(bf16[128,2048]{1,0:T(8,128)(2,1)} %param.12), channel_id=1, source_target_pairs={{0,1},{2,0},{4,2},{6,4},{7,6},{5,7},{3,5},{1,3},{8,9},{10,8},{12,1... | collective-permute-start | bytes 1572872 | tf_op jit(solution)/shard_map/ppermute | solution.py:203
  3.7 26.9 %collective-permute-start.10 = (bf16[128,2048]{1,0:T(8,128)(2,1)}, bf16[128,2048]{1,0:T(8,128)(2,1)S(1)}, u32[]{:S(2)}, u32[]{:S(2)}) collective-permute-start(bf16[128,2048]{1,0:T(8,128)(2,1)} %param.15), channel_id=1, source_target_pairs={{0,2},{2,4},{4,6},{6,7},{7,5},{5,3},{3,1},{1,0},{8,10},{10,12},{12... | collective-permute-start | bytes 1572872 | tf_op jit(solution)/shard_map/ppermute | solution.py:203
  5.7 24.9 %collective-permute-start.11 = (bf16[128,2048]{1,0:T(8,128)(2,1)}, bf16[128,2048]{1,0:T(8,128)(2,1)S(1)}, u32[]{:S(2)}, u32[]{:S(2)}) collective-permute-start(bf16[128,2048]{1,0:T(8,128)(2,1)} %param.15), channel_id=1, source_target_pairs={{0,1},{2,0},{4,2},{6,4},{7,6},{5,7},{3,5},{1,3},{8,9},{10,8},{12,1... | collective-permute-start | bytes 1572872 | tf_op jit(solution)/shard_map/ppermute | solution.py:203
  7.8 20.1 %collective-permute-start = (f32[1,8,128]{2,1,0:T(8,128)S(1)}, f32[1,8,128]{2,1,0:T(8,128)S(1)}, u32[]{:S(2)}, u32[]{:S(2)}) collective-permute-start(f32[1,8,128]{2,1,0:T(8,128)S(1)} %bitcast.173), channel_id=1, source_target_pairs={{0,1},{1,0},{2,3},{3,2},{4,5},{5,4},{6,7},{7,6},{8,9},{9,8},{10,11... | collective-permute-start | bytes 12296 | tf_op jit(solution)/shard_map/ppermute | solution.py:222
  18.8 20.4 %collective-permute-start.4 = (bf16[128,2048]{1,0:T(8,128)(2,1)S(1)}, bf16[128,2048]{1,0:T(8,128)(2,1)S(1)}, u32[]{:S(2)}, u32[]{:S(2)}) collective-permute-start(bf16[128,2048]{1,0:T(8,128)(2,1)S(1)} %collective-permute-done.1), channel_id=1, source_target_pairs={{0,2},{2,4},{4,6},{6,7},{7,5},{5,3},{3,1},{1,0},{8,10},{10,12},{12... | collective-permute-start | bytes 1572872 | tf_op jit(solution)/shard_map/ppermute | solution.py:203
  20.3 20.9 %collective-permute-start.5 = (bf16[128,2048]{1,0:T(8,128)(2,1)S(1)}, bf16[128,2048]{1,0:T(8,128)(2,1)S(1)}, u32[]{:S(2)}, u32[]{:S(2)}) collective-permute-start(bf16[128,2048]{1,0:T(8,128)(2,1)S(1)} %collective-permute-done.2), channel_id=1, source_target_pairs={{0,1},{2,0},{4,2},{6,4},{7,6},{5,7},{3,5},{1,3},{8,9},{10,8},{12,1... | collective-permute-start | bytes 1572872 | tf_op jit(solution)/shard_map/ppermute | solution.py:203
  27.9 15.3 %collective-permute-start.3 = (f32[2,8,128]{2,1,0:T(8,128)S(1)}, f32[2,8,128]{2,1,0:T(8,128)S(1)}, u32[]{:S(2)}, u32[]{:S(2)}) collective-permute-start(f32[2,8,128]{2,1,0:T(8,128)S(1)} %pad_maximum_fusion.14), channel_id=1, source_target_pairs={{0,2},{1,3},{2,0},{3,1},{4,6},{5,7},{6,4},{7,5},{8,10},{9,11},{10,... | collective-permute-start | bytes 24584 | tf_op jit(solution)/shard_map/ppermute | solution.py:222
  30.6 19.8 %collective-permute-start.12 = (bf16[128,2048]{1,0:T(8,128)(2,1)S(1)}, bf16[128,2048]{1,0:T(8,128)(2,1)S(1)}, u32[]{:S(2)}, u32[]{:S(2)}) collective-permute-start(bf16[128,2048]{1,0:T(8,128)(2,1)S(1)} %collective-permute-done.10), channel_id=1, source_target_pairs={{0,2},{2,4},{4,6},{6,7},{7,5},{5,3},{3,1},{1,0},{8,10},{10,12},{12... | collective-permute-start | bytes 1572872 | tf_op jit(solution)/shard_map/ppermute | solution.py:203
  32.5 20.1 %collective-permute-start.13 = (bf16[128,2048]{1,0:T(8,128)(2,1)S(1)}, bf16[128,2048]{1,0:T(8,128)(2,1)S(1)}, u32[]{:S(2)}, u32[]{:S(2)}) collective-permute-start(bf16[128,2048]{1,0:T(8,128)(2,1)S(1)} %collective-permute-done.11), channel_id=1, source_target_pairs={{0,1},{2,0},{4,2},{6,4},{7,6},{5,7},{3,5},{1,3},{8,9},{10,8},{12,1... | collective-permute-start | bytes 1572872 | tf_op jit(solution)/shard_map/ppermute | solution.py:203
  33.0 12.8 %copy-start.8 = (bf16[1,1,2048,384]{3,2,1,0:T(8,128)(2,1)S(1)}, bf16[1,1,2048,384]{3,2,1,0:T(8,128)(2,1)}, u32[]{:S(2)}) copy-start(bf16[1,1,2048,384]{3,2,1,0:T(8,128)(2,1)} %param.17) | copy-start | bytes 4718596
  33.0 12.8 %copy-start.10 = (bf16[1,1,2048,384]{3,2,1,0:T(8,128)(2,1)S(1)}, bf16[1,1,2048,384]{3,2,1,0:T(8,128)(2,1)}, u32[]{:S(2)}) copy-start(bf16[1,1,2048,384]{3,2,1,0:T(8,128)(2,1)} %param.16) | copy-start | bytes 4718596
  41.2 20.4 %collective-permute-start.7 = (bf16[128,2048]{1,0:T(8,128)(2,1)S(1)}, bf16[128,2048]{1,0:T(8,128)(2,1)S(1)}, u32[]{:S(2)}, u32[]{:S(2)}) collective-permute-start(bf16[128,2048]{1,0:T(8,128)(2,1)S(1)} %collective-permute-done.4), channel_id=1, source_target_pairs={{0,2},{2,4},{4,6},{6,7},{7,5},{5,3},{3,1},{1,0},{8,10},{10,12},{12... | collective-permute-start | bytes 1572872 | tf_op jit(solution)/shard_map/ppermute | solution.py:203
  42.8 21.2 %collective-permute-start.8 = (bf16[128,2048]{1,0:T(8,128)(2,1)S(1)}, bf16[128,2048]{1,0:T(8,128)(2,1)S(1)}, u32[]{:S(2)}, u32[]{:S(2)}) collective-permute-start(bf16[128,2048]{1,0:T(8,128)(2,1)S(1)} %collective-permute-done.5), channel_id=1, source_target_pairs={{0,1},{2,0},{4,2},{6,4},{7,6},{5,7},{3,5},{1,3},{8,9},{10,8},{12,1... | collective-permute-start | bytes 1572872 | tf_op jit(solution)/shard_map/ppermute | solution.py:203
  43.3 22.9 %collective-permute-start.6 = (f32[4,8,128]{2,1,0:T(8,128)S(1)}, f32[4,8,128]{2,1,0:T(8,128)S(1)}, u32[]{:S(2)}, u32[]{:S(2)}) collective-permute-start(f32[4,8,128]{2,1,0:T(8,128)S(1)} %pad_maximum_fusion.13), channel_id=1, source_target_pairs={{0,4},{1,5},{2,6},{3,7},{4,0},{5,1},{6,2},{7,3},{8,12},{9,13},{10,... | collective-permute-start | bytes 49160 | tf_op jit(solution)/shard_map/ppermute | solution.py:222
  52.6 21.4 %collective-permute-start.15 = (bf16[128,2048]{1,0:T(8,128)(2,1)S(1)}, bf16[128,2048]{1,0:T(8,128)(2,1)S(1)}, u32[]{:S(2)}, u32[]{:S(2)}) collective-permute-start(bf16[128,2048]{1,0:T(8,128)(2,1)S(1)} %collective-permute-done.13), channel_id=1, source_target_pairs={{0,1},{2,0},{4,2},{6,4},{7,6},{5,7},{3,5},{1,3},{8,9},{10,8},{12,1... | collective-permute-start | bytes 1572872 | tf_op jit(solution)/shard_map/ppermute | solution.py:203
  52.7 20.3 %collective-permute-start.14 = (bf16[128,2048]{1,0:T(8,128)(2,1)S(1)}, bf16[128,2048]{1,0:T(8,128)(2,1)S(1)}, u32[]{:S(2)}, u32[]{:S(2)}) collective-permute-start(bf16[128,2048]{1,0:T(8,128)(2,1)S(1)} %collective-permute-done.12), channel_id=1, source_target_pairs={{0,2},{2,4},{4,6},{6,7},{7,5},{5,3},{3,1},{1,0},{8,10},{10,12},{12... | collective-permute-start | bytes 1572872 | tf_op jit(solution)/shard_map/ppermute | solution.py:203
  64.7 18.6 %collective-permute-start.9 = (bf16[128,2048]{1,0:T(8,128)(2,1)S(1)}, bf16[128,2048]{1,0:T(8,128)(2,1)S(1)}, u32[]{:S(2)}, u32[]{:S(2)}) collective-permute-start(bf16[128,2048]{1,0:T(8,128)(2,1)S(1)} %collective-permute-done.7), channel_id=1, source_target_pairs={{0,2},{2,4},{4,6},{6,7},{7,5},{5,3},{3,1},{1,0},{8,10},{10,12},{12... | collective-permute-start | bytes 1572872 | tf_op jit(solution)/shard_map/ppermute | solution.py:203
  67.0 8.5 %copy-start = (bf16[1,1,384,2048]{3,2,1,0:T(8,128)(2,1)S(1)}, bf16[1,1,384,2048]{3,2,1,0:T(8,128)(2,1)}, u32[]{:S(2)}) copy-start(bf16[1,1,384,2048]{3,2,1,0:T(8,128)(2,1)} %param.18) | copy-start | bytes 4718596
  74.0 12.5 %collective-permute-start.16 = (bf16[128,2048]{1,0:T(8,128)(2,1)S(1)}, bf16[128,2048]{1,0:T(8,128)(2,1)S(1)}, u32[]{:S(2)}, u32[]{:S(2)}) collective-permute-start(bf16[128,2048]{1,0:T(8,128)(2,1)S(1)} %collective-permute-done.15), channel_id=1, source_target_pairs={{0,1},{2,0},{4,2},{6,4},{7,6},{5,7},{3,5},{1,3},{8,9},{10,8},{12,1... | collective-permute-start | bytes 1572872 | tf_op jit(solution)/shard_map/ppermute | solution.py:203
  90.9 21.9 %collective-permute-start.19 = (bf16[384,2048]{1,0:T(8,128)(2,1)S(1)}, bf16[384,2048]{1,0:T(8,128)(2,1)S(1)}, u32[]{:S(2)}, u32[]{:S(2)}) collective-permute-start(bf16[384,2048]{1,0:T(8,128)(2,1)S(1)} %get-tuple-element.139), channel_id=1, source_target_pairs={{0,8},{8,0},{16,24},{24,16},{1,9},{9,1},{17,25},{25,17},{2,10},{10... | collective-permute-start | bytes 4718600 | tf_op jit(solution)/shard_map/ppermute | solution.py:13
  90.9 37.2 %collective-permute-start.22 = (bf16[384,2048]{1,0:T(8,128)(2,1)S(1)}, bf16[384,2048]{1,0:T(8,128)(2,1)S(1)}, u32[]{:S(2)}, u32[]{:S(2)}) collective-permute-start(bf16[384,2048]{1,0:T(8,128)(2,1)S(1)} %get-tuple-element.139), channel_id=1, source_target_pairs={{0,16},{8,24},{16,0},{24,8},{1,17},{9,25},{17,1},{25,9},{2,18},{10... | collective-permute-start | bytes 4718600 | tf_op jit(solution)/shard_map/ppermute | solution.py:13
  94.0 18.3 %collective-permute-start.18 = (bf16[128,2048]{1,0:T(8,128)(2,1)S(1)}, bf16[128,2048]{1,0:T(8,128)(2,1)S(1)}, u32[]{:S(2)}, u32[]{:S(2)}) collective-permute-start(bf16[128,2048]{1,0:T(8,128)(2,1)S(1)} %convolution_multiply_fusion.14), channel_id=1, source_target_pairs={{0,1},{2,0},{4,2},{6,4},{7,6},{5,7},{3,5},{1,3},{8,9},{10,8},{12,1... | collective-permute-start | bytes 1572872 | tf_op jit(solution)/shard_map/ppermute | solution.py:203
  94.6 17.9 %collective-permute-start.17 = (bf16[128,2048]{1,0:T(8,128)(2,1)S(1)}, bf16[128,2048]{1,0:T(8,128)(2,1)S(1)}, u32[]{:S(2)}, u32[]{:S(2)}) collective-permute-start(bf16[128,2048]{1,0:T(8,128)(2,1)S(1)} %convolution_multiply_fusion.15), channel_id=1, source_target_pairs={{0,2},{2,4},{4,6},{6,7},{7,5},{5,3},{3,1},{1,0},{8,10},{10,12},{12... | collective-permute-start | bytes 1572872 | tf_op jit(solution)/shard_map/ppermute | solution.py:203
  104.1 91.0 %collective-permute-start.28 = (bf16[4096,384]{1,0:T(8,128)(2,1)S(1)}, bf16[4096,384]{1,0:T(8,128)(2,1)S(1)}, u32[]{:S(2)}, u32[]{:S(2)}) collective-permute-start(bf16[4096,384]{1,0:T(8,128)(2,1)S(1)} %pad_maximum_fusion.1), channel_id=1, source_target_pairs={{0,16},{8,24},{16,0},{24,8},{1,17},{9,25},{17,1},{25,9},{2,18},{10... | collective-permute-start | bytes 9437192 | tf_op jit(solution)/shard_map/ppermute | solution.py:13
  112.7 24.8 %collective-permute-start.21 = (bf16[256,2048]{1,0:T(8,128)(2,1)S(1)}, bf16[256,2048]{1,0:T(8,128)(2,1)S(1)}, u32[]{:S(2)}, u32[]{:S(2)}) collective-permute-start(bf16[256,2048]{1,0:T(8,128)(2,1)S(1)} %pad_maximum_fusion.3), channel_id=1, source_target_pairs={{0,1},{2,0},{4,2},{6,4},{7,6},{5,7},{3,5},{1,3},{8,9},{10,8},{12,1... | collective-permute-start | bytes 3145736 | tf_op jit(solution)/shard_map/ppermute | solution.py:203
  114.6 24.6 %collective-permute-start.20 = (bf16[256,2048]{1,0:T(8,128)(2,1)S(1)}, bf16[256,2048]{1,0:T(8,128)(2,1)S(1)}, u32[]{:S(2)}, u32[]{:S(2)}) collective-permute-start(bf16[256,2048]{1,0:T(8,128)(2,1)S(1)} %pad_maximum_fusion.2), channel_id=1, source_target_pairs={{0,2},{2,4},{4,6},{6,7},{7,5},{5,3},{3,1},{1,0},{8,10},{10,12},{12... | collective-permute-start | bytes 3145736 | tf_op jit(solution)/shard_map/ppermute | solution.py:203
  128.1 39.2 %collective-permute-start.27 = (bf16[4096,384]{1,0:T(8,128)(2,1)S(1)}, bf16[4096,384]{1,0:T(8,128)(2,1)S(1)}, u32[]{:S(2)}, u32[]{:S(2)}) collective-permute-start(bf16[4096,384]{1,0:T(8,128)(2,1)S(1)} %pad_maximum_fusion.1), channel_id=1, source_target_pairs={{0,8},{8,0},{16,24},{24,16},{1,9},{9,1},{17,25},{25,17},{2,10},{10... | collective-permute-start | bytes 9437192 | tf_op jit(solution)/shard_map/ppermute | solution.py:13
  139.5 23.6 %collective-permute-start.24 = (bf16[256,2048]{1,0:T(8,128)(2,1)S(1)}, bf16[256,2048]{1,0:T(8,128)(2,1)S(1)}, u32[]{:S(2)}, u32[]{:S(2)}) collective-permute-start(bf16[256,2048]{1,0:T(8,128)(2,1)S(1)} %fusion.9), channel_id=1, source_target_pairs={{0,1},{2,0},{4,2},{6,4},{7,6},{5,7},{3,5},{1,3},{8,9},{10,8},{12,1... | collective-permute-start | bytes 3145736 | tf_op jit(solution)/shard_map/ppermute | solution.py:203
  141.8 23.0 %collective-permute-start.23 = (bf16[256,2048]{1,0:T(8,128)(2,1)S(1)}, bf16[256,2048]{1,0:T(8,128)(2,1)S(1)}, u32[]{:S(2)}, u32[]{:S(2)}) collective-permute-start(bf16[256,2048]{1,0:T(8,128)(2,1)S(1)} %fusion.8), channel_id=1, source_target_pairs={{0,2},{2,4},{4,6},{6,7},{7,5},{5,3},{3,1},{1,0},{8,10},{10,12},{12... | collective-permute-start | bytes 3145736 | tf_op jit(solution)/shard_map/ppermute | solution.py:203
  165.2 22.2 %collective-permute-start.25 = (bf16[256,2048]{1,0:T(8,128)(2,1)S(1)}, bf16[256,2048]{1,0:T(8,128)(2,1)S(1)}, u32[]{:S(2)}, u32[]{:S(2)}) collective-permute-start(bf16[256,2048]{1,0:T(8,128)(2,1)S(1)} %fusion.7), channel_id=1, source_target_pairs={{0,2},{2,4},{4,6},{6,7},{7,5},{5,3},{3,1},{1,0},{8,10},{10,12},{12... | collective-permute-start | bytes 3145736 | tf_op jit(solution)/shard_map/ppermute | solution.py:203
  165.8 22.0 %collective-permute-start.26 = (bf16[256,2048]{1,0:T(8,128)(2,1)S(1)}, bf16[256,2048]{1,0:T(8,128)(2,1)S(1)}, u32[]{:S(2)}, u32[]{:S(2)}) collective-permute-start(bf16[256,2048]{1,0:T(8,128)(2,1)S(1)} %fusion.10), channel_id=1, source_target_pairs={{0,1},{2,0},{4,2},{6,4},{7,6},{5,7},{3,5},{1,3},{8,9},{10,8},{12,1... | collective-permute-start | bytes 3145736 | tf_op jit(solution)/shard_map/ppermute | solution.py:203
  (9 other events, 33.6 us)
